TPU v7x, 32 devices: a whole 2x2x4 slice. The times are simulated.
32 devices in a mesh: dp: 16 (over z, x, core), tensor: 2 (over y).
Axes of the slice: x: 2, y: 2, z: 4, core: 2. Of those that a mesh axis runs over, the one named last changes fastest.
Arguments:
- inputs: bfloat16 [32, 1024, 768], P(('dp', 'tensor')), may hold values from -6 to 6
- prenorm: float32 [768], replicated, may hold values from 0.5 to 1.5
- gate_weight: bfloat16 [768, 1536], P('dp', 'tensor'), may hold values from -0.21875 to 0.21875
- value_weight: bfloat16 [768, 1536], P('dp', 'tensor'), may hold values from -0.21875 to 0.21875
- state_weight: bfloat16 [768, 256], P('dp'), may hold values from -0.21875 to 0.21875
- step_weight: bfloat16 [768, 24], P('dp', 'tensor'), may hold values from -0.21875 to 0.21875
- value_conv: float32 [4, 1536], P(None, 'tensor'), may hold values from -3 to 3
- value_shift: float32 [1536], P('tensor'), may hold values from -3 to 3
- state_conv: float32 [4, 256], replicated, may hold values from -3 to 3
- state_shift: float32 [256], replicated, may hold values from -3 to 3
- step_shift: float32 [24], P('tensor'), may hold values from -6.5 to -2.5
- decay_log: float32 [24], P('tensor'), may hold values from 0 to 2.7
- skip_scale: float32 [24], P('tensor'), may hold values from 0.5 to 1.5
- gated_gain: float32 [1536], P('tensor'), may hold values from 0.5 to 1.5
- output_matrix: bfloat16 [1536, 768], P('tensor', 'dp'), may hold values from -0.15625 to 0.15625
- cotangent: bfloat16 [32, 1024, 768], P(('dp', 'tensor')), may hold values from -6 to 6
Outputs:
- result: bfloat16 [32, 1024, 768], P(('dp', 'tensor'))
- input_grad: float32 [32, 1024, 768], P(('dp', 'tensor'))
- prenorm_grad: float32 [768], replicated
- gate_grad: float32 [768, 1536], P('dp', 'tensor')
- value_grad: float32 [768, 1536], P('dp', 'tensor')
- state_grad: float32 [768, 256], P('dp')
- step_grad: float32 [768, 24], P('dp', 'tensor')
- valueconv_grad: float32 [4, 1536], P(None, 'tensor')
- valueshift_grad: float32 [1536], P('tensor')
- stateconv_grad: float32 [4, 256], replicated
- stateshift_grad: float32 [256], replicated
- stepshift_grad: float32 [24], P('tensor')
- decay_grad: float32 [24], P('tensor')
- skip_grad: float32 [24], P('tensor')
- gated_grad: float32 [1536], P('tensor')
- out_grad: float32 [1536, 768], P('tensor', 'dp')
All inputs are finite; a program needn't handle non-finite values.
Results may differ from a plain program's by a relative error of at most 0.0078.
Values may be sent and summed in bfloat16 or wider, within the bound.
No kernel may reach another device: no remote copies, remote signals or barrier semaphores. Data moves between devices by JAX's collectives and lax.ppermute only.
A program may use at most 192 MiB of HBM per device.

v0:
```python
import jax
import jax.numpy as jnp
from jax import lax
from jax.sharding import PartitionSpec as P

BLOCK = 256


exact_precision = lax.Precision.HIGHEST
epsilon = 1e-05


def causal_conv(signal, kernel, shift):
    taps = kernel.shape[0]
    length = signal.shape[1]
    padded = jnp.pad(signal, ((0, 0), (taps - 1, 0), (0, 0)))
    total = shift + jnp.zeros_like(signal)
    for offset in range(taps):
        total = total + kernel[offset] * padded[:, offset : offset + length, :]
    return total


def ssd_scan(values, step_sizes, decay_rates, write_map, read_map, skip_scale):
    sequences, positions, head_count, head_width = values.shape
    blocks = positions // BLOCK

    def split(array):
        return jnp.moveaxis(array.reshape((sequences, blocks, BLOCK) + array.shape[2:]), 1, 0)

    causal = (jnp.arange(BLOCK)[:, None] >= jnp.arange(BLOCK)[None, :])[None, None]

    def advance(state, block):
        value_blk, step_blk, write_blk, read_blk = block
        logged = jnp.cumsum(jnp.swapaxes(step_blk * decay_rates, 1, 2), axis=2)
        grams = jnp.einsum("sqn,skn->sqk", read_blk, write_blk, precision=exact_precision)
        spread_log = logged[:, :, :, None] - logged[:, :, None, :]
        decay = jnp.where(causal, jnp.exp(jnp.where(causal, spread_log, 0.0)), 0.0)
        mixing = grams[:, None] * decay * jnp.swapaxes(step_blk, 1, 2)[:, :, None, :]
        within = jnp.einsum("shqk,skhp->sqhp", mixing, value_blk, precision=exact_precision)
        carried = jnp.einsum("sqn,shpn->sqhp", read_blk, state, precision=exact_precision)
        carried = carried * jnp.swapaxes(jnp.exp(logged), 1, 2)[..., None]
        remain = jnp.swapaxes(jnp.exp(logged[:, :, -1:] - logged), 1, 2) * step_blk
        update = jnp.einsum(
            "skn,skhp->shpn", write_blk, value_blk * remain[..., None], precision=exact_precision
        )
        state = state * jnp.exp(logged[:, :, -1])[:, :, None, None] + update
        return (state, within + carried)

    initial = jnp.zeros((sequences, head_count, head_width, write_map.shape[-1]), jnp.float32)
    _, mixed = lax.scan(
        jax.checkpoint(advance),
        initial,
        (split(values), split(step_sizes), split(write_map), split(read_map)),
    )
    mixed = jnp.moveaxis(mixed, 0, 1).reshape(values.shape)
    return mixed + skip_scale[:, None] * values


def head_mixer(
    value_in,
    write_map,
    read_map,
    step_raw,
    gate_in,
    value_conv,
    value_shift,
    step_shift,
    decay_log,
    skip_scale,
):
    values = jax.nn.silu(causal_conv(value_in, value_conv, value_shift))
    step_sizes = jax.nn.softplus(step_raw + step_shift)
    sequences, positions, channels = values.shape
    head_count = step_sizes.shape[-1]
    mixed = ssd_scan(
        values.reshape(sequences, positions, head_count, channels // head_count),
        step_sizes,
        -jnp.exp(decay_log),
        write_map,
        read_map,
        skip_scale,
    )
    return mixed.reshape(values.shape) * jax.nn.silu(gate_in)


def state_inputs(state_in, state_conv, state_shift):
    active = jax.nn.silu(causal_conv(state_in, state_conv, state_shift))
    half = active.shape[-1] // 2
    return (active[..., :half], active[..., half:])


def widen(slice_portion, place, parts):
    full = jnp.zeros(slice_portion.shape[:-1] + (slice_portion.shape[-1] * parts,), jnp.float32)
    return lax.dynamic_update_slice_in_dim(
        full, slice_portion, place * slice_portion.shape[-1], slice_portion.ndim - 1
    )


def narrow(whole, place, parts):
    length = whole.shape[-1] // parts
    return lax.dynamic_slice_in_dim(whole, place * length, length, whole.ndim - 1)


def local(
    inputs,
    prenorm,
    gate_weight,
    value_weight,
    state_weight,
    step_weight,
    value_conv,
    value_shift,
    state_conv,
    state_shift,
    step_shift,
    decay_log,
    skip_scale,
    gated_gain,
    output_matrix,
    cotangent,
):
    parts = lax.axis_size("tensor")
    place = lax.axis_index("tensor")
    own_seqs = inputs.shape[0]
    channels = gate_weight.shape[1]
    head_count = step_weight.shape[1]
    full_gate, full_value, complete_state, full_step, complete_output = (
        lax.all_gather(gate_weight, "dp", axis=0, tiled=True),
        lax.all_gather(value_weight, "dp", axis=0, tiled=True),
        lax.all_gather(state_weight, "dp", axis=0, tiled=True),
        lax.all_gather(step_weight, "dp", axis=0, tiled=True),
        lax.all_gather(output_matrix, "dp", axis=1, tiled=True),
    )
    token_rows = inputs.astype(jnp.float32)
    inv_rms = lax.rsqrt(jnp.mean(token_rows * token_rows, axis=-1, keepdims=True) + epsilon)
    normalized_input = (token_rows * inv_rms * prenorm).astype(jnp.bfloat16)
    leading_part = jnp.concatenate([full_gate, full_value, full_step], axis=1)
    collected_parts = lax.all_gather(normalized_input, "tensor", axis=0, tiled=True)
    projected = jnp.einsum(
        "bzj,jf->bzf",
        collected_parts,
        jnp.concatenate([leading_part, complete_state], axis=1),
        preferred_element_type=jnp.float32,
    )
    gate_in = projected[..., :channels]
    value_in = projected[..., channels : 2 * channels]
    step_raw = projected[..., 2 * channels : 2 * channels + head_count]
    state_in = projected[..., 2 * channels + head_count :]
    (write_map, read_map), state_pull = jax.vjp(state_inputs, state_in, state_conv, state_shift)
    mixed, mixer_pull = jax.vjp(
        head_mixer,
        value_in,
        write_map,
        read_map,
        step_raw,
        gate_in,
        value_conv,
        value_shift,
        step_shift,
        decay_log,
        skip_scale,
    )
    squares = lax.psum(jnp.sum(mixed * mixed, axis=-1, keepdims=True), "tensor")
    gate_rms = lax.rsqrt(squares / (channels * parts) + epsilon)
    scaled = mixed * gate_rms
    gated_result = (scaled * gated_gain).astype(jnp.bfloat16)
    own_gated = lax.all_to_all(gated_result, "tensor", split_axis=0, concat_axis=2, tiled=True)
    every_out, every_front = (
        lax.all_gather(complete_output, "tensor", axis=0, tiled=True),
        lax.all_gather(leading_part, "tensor", axis=1, tiled=True),
    )
    mixer = jnp.einsum("kmt,tz->kmz", own_gated, every_out, preferred_element_type=jnp.float32)
    result = (token_rows + mixer).astype(jnp.bfloat16)
    slice_portion = lax.all_gather(cotangent, "tensor", axis=0, tiled=True)
    matrix_product = jnp.einsum(
        "nzk,bk->nzb", slice_portion, complete_output, preferred_element_type=jnp.float32
    )
    output_accumulator = jnp.einsum(
        "zwj,zwh->jh", gated_result, slice_portion, preferred_element_type=jnp.float32
    )
    grad_scaled = matrix_product * gated_gain
    inner = lax.psum(jnp.sum(grad_scaled * mixed, axis=-1, keepdims=True), "tensor")
    grad_mixed = gate_rms * grad_scaled - mixed * gate_rms**3 * inner / (channels * parts)
    gated_part = jnp.sum(matrix_product * scaled, axis=(0, 1))
    (
        grad_value,
        grad_write,
        grad_read,
        grad_step,
        grad_gate,
        conv_value,
        shift_value,
        shift_step,
        decay_sum,
        skip_sum,
    ) = mixer_pull(grad_mixed)
    grad_write, grad_read = lax.psum((grad_write, grad_read), "tensor")
    grad_state, conv_state, shift_state = state_pull((grad_write, grad_read))
    device_gradients = jnp.concatenate([grad_gate, grad_value, grad_step], axis=-1).astype(
        jnp.bfloat16
    )
    state_reduced = grad_state.astype(jnp.bfloat16)
    own_grads = lax.all_to_all(device_gradients, "tensor", split_axis=0, concat_axis=2, tiled=True)
    grad_normed = jnp.einsum(
        "qub,tb->qut", own_grads, every_front, preferred_element_type=jnp.float32
    )
    own_portion = lax.dynamic_slice_in_dim(state_reduced, place * own_seqs, own_seqs, 0)
    grad_normed = grad_normed + jnp.einsum(
        "qub,tb->qut", own_portion, complete_state, preferred_element_type=jnp.float32
    )
    device_partial_sum = jnp.einsum(
        "veb,vez->bz", collected_parts, device_gradients, preferred_element_type=jnp.float32
    )
    lead_device = (place == 0).astype(jnp.float32)
    state_sum = (
        jnp.einsum(
            "veb,vez->bz", collected_parts, state_reduced, preferred_element_type=jnp.float32
        )
        * lead_device
    )
    gate_sum = device_partial_sum[:, :channels]
    value_sum = device_partial_sum[:, channels : 2 * channels]
    step_sum = device_partial_sum[:, 2 * channels :]
    small = (
        widen(conv_value, place, parts),
        widen(shift_value, place, parts),
        widen(shift_step, place, parts),
        widen(decay_sum, place, parts),
        widen(skip_sum, place, parts),
        widen(gated_part, place, parts),
        conv_state * lead_device,
        shift_state * lead_device,
    )
    grad_gain = grad_normed * prenorm
    input_grad = (
        cotangent.astype(jnp.float32)
        + inv_rms * grad_gain
        - token_rows * inv_rms**3 * jnp.mean(grad_gain * token_rows, axis=-1, keepdims=True)
    )
    prenorm_part = jnp.sum(grad_normed * token_rows * inv_rms, axis=(0, 1))
    gate_grad, value_grad, step_grad, out_grad = (
        lax.psum_scatter(gate_sum, "dp", scatter_dimension=0, tiled=True),
        lax.psum_scatter(value_sum, "dp", scatter_dimension=0, tiled=True),
        lax.psum_scatter(step_sum, "dp", scatter_dimension=0, tiled=True),
        lax.psum_scatter(output_accumulator, "dp", scatter_dimension=1, tiled=True),
    )
    summed = lax.psum(
        (
            small[0],
            small[1],
            small[2],
            small[3],
            small[4],
            small[5],
            small[6],
            small[7],
            state_sum,
            prenorm_part,
        ),
        ("dp", "tensor"),
    )
    conv_value = narrow(summed[0], place, parts)
    shift_value = narrow(summed[1], place, parts)
    shift_step = narrow(summed[2], place, parts)
    decay_sum = narrow(summed[3], place, parts)
    skip_sum = narrow(summed[4], place, parts)
    gated_part = narrow(summed[5], place, parts)
    conv_state = summed[6]
    shift_state = summed[7]
    row_count = gate_grad.shape[0]
    state_grad = lax.dynamic_slice_in_dim(summed[8], lax.axis_index("dp") * row_count, row_count, 0)
    prenorm_grad = summed[9]
    return (
        result,
        input_grad,
        prenorm_grad,
        gate_grad,
        value_grad,
        state_grad,
        step_grad,
        conv_value,
        shift_value,
        conv_state,
        shift_state,
        shift_step,
        decay_sum,
        skip_sum,
        gated_part,
        out_grad,
    )


def solution(mesh):
    in_specs = (
        P(("dp", "tensor"), None, None),
        P(),
        P("dp", "tensor"),
        P("dp", "tensor"),
        P("dp", None),
        P("dp", "tensor"),
        P(None, "tensor"),
        P("tensor"),
        P(),
        P(),
        P("tensor"),
        P("tensor"),
        P("tensor"),
        P("tensor"),
        P("tensor", "dp"),
        P(("dp", "tensor"), None, None),
    )
    out_specs = (
        P(("dp", "tensor"), None, None),
        P(("dp", "tensor"), None, None),
        P(),
        P("dp", "tensor"),
        P("dp", "tensor"),
        P("dp", None),
        P("dp", "tensor"),
        P(None, "tensor"),
        P("tensor"),
        P(),
        P(),
        P("tensor"),
        P("tensor"),
        P("tensor"),
        P("tensor"),
        P("tensor", "dp"),
    )
    return jax.shard_map(local, mesh=mesh, in_specs=in_specs, out_specs=out_specs, check_vma=False)
```

profile of v0, /device:TPU:0, one launch (start us, length us, event | category | flops | bytes accessed | tf_op | source)
XLA Modules:
  0.0 1277.8 jit_solution(363135484314260784)
XLA Ops:
  18.6 23.3 %all-gather = bf16[16,48,12]{1,2,0:T(8,128)(2,1)S(1)} all-gather(bf16[1,48,12]{1,2,0:T(8,128)(2,1)S(1)} %bitcast.431), channel_id=1, replica_groups=mesh['dp'=16,'tensor'=2] {'dp'}, dimensions={0}, use_global_device_ids=true | all-gather | bytes 19584 | tf_op jit(solution)/shard_map/all_gather | solution.py:131
  42.6 18.7 %all_gather.31 = bf16[768,256]{1,0:T(8,128)(2,1)S(1)} all-gather(bf16[48,256]{1,0:T(8,128)(2,1)S(1)} %copy-done.42), channel_id=1, replica_groups=mesh['dp'=16,'tensor'=2] {'dp'}, dimensions={0}, use_global_device_ids=true | all-gather | bytes 417792 | tf_op jit(solution)/shard_map/all_gather | solution.py:130
  63.6 27.4 %all-gather.12.cloned.1.call-done = bf16[768,768]{1,0:T(8,128)(2,1)} async-done(((bf16[48,768]{1,0:T(8,128)(2,1)}), bf16[768,768]{1,0:T(8,128)(2,1)}) %all-gather.12.cloned.1.call-update) | async-done | bytes 1179664 | tf_op jit(solution)/shard_map/all_gather | solution.py:128
  92.6 11.0 concatenate.11
  103.6 33.5 %all-gather.10.cloned.1.call-done = bf16[2,1024,768]{2,1,0:T(8,128)(2,1)} async-done(((bf16[1,1024,768]{2,1,0:T(8,128)(2,1)}), bf16[2,1024,768]{2,1,0:T(8,128)(2,1)}) %all-gather.10.cloned.1.call-update) | async-done | bytes 3145744 | tf_op jit(solution)/shard_map/all_gather | solution.py:138
  137.1 9.0 fusion.115
  163.1 16.4 %fusion.104 = (f32[2,1024,768]{1,2,0:T(8,128)}, f32[2,1024,768]{1,2,0:T(8,128)}) fusion(f32[2,1024,768]{1,2,0:T(8,128)} %slice.181, f32[768]{0:T(1024)S(1)} %copy-done.38, f32[768]{0:T(1024)S(1)} %copy-done.40, f32[768]{0:T(1024)S(1)} %get-tuple-element.804, f32[768]{0:T(1024)S(1)} %get-tuple-element.803, f32[768]{0:T(1024)S(1)} %copy-done.58), kind=kLoop, calls=%fused_computation.170 | loop fusion | flops 18874368 | bytes 18889728 | tf_op jit(solution)/shard_map/jvp(jit(silu))/mul | solution.py:71
  179.5 8.6 reshape.419
  188.1 6.8 copy.363
  198.3 80.6 %while.44 = (s32[]{:T(128)}, f32[2,12,64,128]{3,2,1,0:T(8,128)S(1)}, f32[4,2,256,12,64]{2,4,3,1,0:T(8,128)}, f32[4,2,12,64,128]{4,3,2,1,0:T(8,128)}, f32[4,2,256...) while((s32[]{:T(128)}, ...), condition=%wide.region_4.5_spmd.clone.clone, body=%wide.region_1.4_spmd.clone.clone.sunk | while | flops 2628077568 | bytes 14875187 | solution.py:50
  202.1 8.7 fusion.247
  222.2 8.7 fusion.247
  242.3 8.7 fusion.247
  262.4 8.7 fusion.247
  278.9 10.4 copy.307
  289.3 8.3 reshape.422
  297.6 10.0 multiply_reduce_fusion.12
  312.7 10.7 multiply_reduce_fusion.5
  328.4 20.2 %multiply_reduce_fusion.6 = (f32[768]{0:T(1024)}, f32[2,1024,768]{1,2,0:T(8,128)}, bf16[2,1024,768]{1,2,0:T(8,128)(2,1)}, bf16[2,1024,768]{1,2,0:T(8,128)(2,1)}) fusion(f32[2,1024,768]{1,2,0:T(8,128)} %get-tuple-element.875, f32[2,1024,1804]{1,2,0:T(8,128)} %copy-done.2, f32[2,1024]{1,0:T(2,128)S(1)} %psum.99, f32[2,1024,768]{1,2,0:T(8,128)} %get-tuple-element.871, ...), kind=kLoop, calls=%fused_computation.157 | loop fusion | flops 47185152 | bytes 44073984 | tf_op jit(solution)/shard_map/transpose(jvp())/reduce_sum | solution.py:56
  348.5 8.1 reshape.424
  356.6 6.6 copy.362
  370.0 316.6 %while.43 = (s32[]{:T(128)}, f32[12]{0:T(128)}, f32[2,12,64,128]{3,2,1,0:T(8,128)}, f32[4,2,256,12,64]{2,4,3,1,0:T(8,128)}, f32[4,2,256,12]{3,1,2,0:T(2,128)}, /...) while((s32[]{:T(128)}, f32[12]{0:T(128)}, ...), condition=%wide.region_23.24_spmd.clone, body=%wide.region_9.23_spmd.clone.sunk | while | flops 6077532160 | bytes 57636632 | solution.py:50
  388.9 12.7 fusion.227
  441.6 6.7 bitcast_dynamic-update-slice_fusion.8
  468.2 12.7 fusion.227
  520.9 6.7 bitcast_dynamic-update-slice_fusion.8
  547.5 12.7 fusion.227
  600.2 6.7 bitcast_dynamic-update-slice_fusion.8
  626.8 12.7 fusion.227
  679.4 6.7 bitcast_dynamic-update-slice_fusion.8
  694.1 10.4 copy.311
  704.5 8.4 reshape.425
  712.9 16.6 %multiply_reduce_fusion.9 = (f32[768]{0:T(1024)S(1)}, f32[768]{0:T(1024)S(1)}, f32[768]{0:T(1024)S(1)}, f32[768]{0:T(1024)S(1)}, f32[768]{0:T(1024)S(1)}, /*index=5*/f32[2,1024,768]{1,2,0:T(8,128)S(1)}) fusion(f32[2,1024,768]{1,2,0:T(8,128)} %slice.181, f32[2,1024,1804]{1,2,0:T(8,128)} %copy-done.2, f32[2,1024,768]{1,2,0:T(8,128)} %get-tuple-element.875, ...), kind=kLoop, calls=%fused_computation.160 | loop fusion | flops 31453440 | bytes 37767168 | tf_op jit(solution)/shard_map/transpose(jvp())/reduce_sum | solution.py:19
  735.4 9.3 fusion.102
  744.7 8.7 convolution_bitcast_fusion
  772.6 7.0 convolution_bitcast_fusion.1
  791.3 8.8 pad_maximum_fusion
  800.0 27.5 %all-to-all-done = bf16[2,1024,768]{1,2,0:T(8,128)(2,1)} async-done(((bf16[2,1024,768]{1,2,0:T(8,128)(2,1)}), bf16[2,1024,768]{1,2,0:T(8,128)(2,1)}, u32[]{:S(2)}, u32[]{:S(2)}) %all-to-all-start) | async-done | bytes 3145760 | tf_op jit(solution)/shard_map/all_to_all | solution.py:167
  827.5 6.5 all-to-all-start.1
  840.2 31.7 %all-gather.18.cloned.1.call-done = bf16[1536,768]{0,1:T(8,128)(2,1)} async-done(((bf16[768,768]{0,1:T(8,128)(2,1)}), bf16[1536,768]{0,1:T(8,128)(2,1)}) %all-gather.18.cloned.1.call-update) | async-done | bytes 2359312 | tf_op jit(solution)/shard_map/all_gather | solution.py:169
  871.9 6.4 fusion.108
  878.3 128.1 %all-reduce.26.cloned.1.call-done = f32[768,256]{1,0:T(8,128)} async-done(((f32[768,256]{1,0:T(8,128)}), f32[768,256]{1,0:T(8,128)}) %all-reduce.26.cloned.1.call-update) | async-done | bytes 786448 | tf_op jit(solution)/shard_map/psum | solution.py:247
  1007.9 7.1 reshape.427
  1015.0 55.2 %all-gather.22.cloned.1.call-done = bf16[2,1548,768]{2,1,0:T(8,128)(2,1)} async-done(((bf16[1,1548,768]{2,1,0:T(8,128)(2,1)}), bf16[2,1548,768]{2,1,0:T(8,128)(2,1)}) %all-gather.22.cloned.1.call-update) | async-done | bytes 4755472 | tf_op jit(solution)/shard_map/all_gather | solution.py:170
  1075.6 9.2 fusion.144
  1087.7 41.2 %all-reduce.22 = (f32[768]{0:T(1024)}, f32[4,1536]{1,0:T(4,128)S(1)}, f32[1536]{0:T(1024)S(1)}, f32[4,256]{1,0:T(4,128)}, f32[256]{0:T(256)}, /*index=5*/f32[24]...) all-reduce(f32[768]{0:T(1024)S(1)} %get-tuple-element.796, ...), channel_id=1, replica_groups=mesh['dp'=16,'tensor'=2] {'dp','tensor'}, use_global_device_ids=true, to_apply=%region_28.29 | all-reduce | flops 11336 | bytes 90688 | tf_op jit(solution)/shard_map/psum | solution.py:247
  1138.0 66.2 %reduce-scatter.15.cloned.1.call-done = f32[48,768]{1,0:T(8,128)} async-done(((f32[768,768]{1,0:T(8,128)}), f32[48,768]{1,0:T(8,128)}) %reduce-scatter.15.cloned.1.call-update) | async-done | bytes 147472
  1204.2 66.8 %reduce-scatter.13.cloned.1.call-done = f32[48,768]{1,0:T(8,128)} async-done(((f32[768,768]{1,0:T(8,128)}), f32[48,768]{1,0:T(8,128)}) %reduce-scatter.13.cloned.1.call-update) | async-done | bytes 147472
  (646 shorter events, 404.5 us)
Async XLA Ops:
  7.2 35.4 %copy-start.42 = (bf16[48,256]{1,0:T(8,128)(2,1)S(1)}, bf16[48,256]{1,0:T(8,128)(2,1)}, u32[]{:S(2)}) copy-start(bf16[48,256]{1,0:T(8,128)(2,1)} %param.24) | copy-start | bytes 73732
  7.2 54.8 %all-gather.14.cloned.1.call-start = ((), (), s32[]{:S(2)}) async-start(), calls=%async_computation.8 | async-start | bytes 1253376 | tf_op jit(solution)/shard_map/all_gather | solution.py:129
  8.0 83.1 %all-gather.12.cloned.1.call-start = ((), (), s32[]{:S(2)}) async-start(), calls=%async_computation.7 | async-start | bytes 1253376 | tf_op jit(solution)/shard_map/all_gather | solution.py:128
  8.7 128.4 %all-gather.10.cloned.1.call-start = ((), (), s32[]{:S(2)}) async-start(), calls=%async_computation.6 | async-start | bytes 4718592 | tf_op jit(solution)/shard_map/all_gather | solution.py:138
  14.8 297.9 %all-gather.16.cloned.1.call-start = ((), (), s32[]{:S(2)}) async-start(), calls=%async_computation.9 | async-start | bytes 1253376 | tf_op jit(solution)/shard_map/all_gather | solution.py:132
  15.3 297.3 %all-gather.20.cloned.1.call-start = ((), (), s32[]{:S(2)}) async-start(), calls=%async_computation.11 | async-start | bytes 4718592 | tf_op jit(solution)/shard_map/all_gather | solution.py:174
  15.9 741.5 %all-reduce.28.cloned.1.call-start = ((), (), s32[]{:S(2)}) async-start(), calls=%async_computation.14 | async-start | bytes 4194304 | tf_op jit(solution)/shard_map/psum | solution.py:197
  17.9 310.4 %copy-start.28 = (f32[768]{0:T(1024)}, f32[768]{0:T(1024)S(1)}, u32[]{:S(2)}) copy-start(f32[768]{0:T(1024)S(1)} %mul.839) | copy-start | bytes 9220
  18.5 144.5 %copy-start.34 = (f32[768]{0:T(1024)}, f32[768]{0:T(1024)S(1)}, u32[]{:S(2)}) copy-start(f32[768]{0:T(1024)S(1)} %get-tuple-element.803) | copy-start | bytes 9220
  18.5 144.5 %copy-start.36 = (f32[768]{0:T(1024)}, f32[768]{0:T(1024)S(1)}, u32[]{:S(2)}) copy-start(f32[768]{0:T(1024)S(1)} %get-tuple-element.804) | copy-start | bytes 9220
  297.6 15.1 %copy-start.59 = (f32[768]{0:T(1024)S(1)}, f32[768]{0:T(1024)}, u32[]{:S(2)}) copy-start(f32[768]{0:T(1024)} %param.33) | copy-start | bytes 9220
  388.9 12.7 copy-start.8
  409.1 18.7 %copy-start.43 = (f32[12]{0:T(128)S(1)}, f32[12]{0:T(128)}, u32[]{:S(2)}) copy-start(f32[12]{0:T(128)} %get-tuple-element.1173) | copy-start | bytes 148 | tf_op jit(solution)/shard_map/transpose(jvp())/while
  425.4 13.0 %copy-start.1 = (f32[2,256,128]{2,1,0:T(8,128)S(1)}, f32[2,256,128]{2,1,0:T(8,128)}, u32[]{:S(2)}) copy-start(f32[2,256,128]{2,1,0:T(8,128)} %get-tuple-element.1086) | copy-start | bytes 786436 | tf_op jit(solution)/shard_map/transpose(jvp())/while
  427.8 13.7 %copy-start.44 = (f32[12]{0:T(128)}, f32[12]{0:T(128)S(1)}, u32[]{:S(2)}) copy-start(f32[12]{0:T(128)S(1)} %fusion.230) | copy-start | bytes 148 | tf_op jit(solution)/shard_map/transpose(jvp())/while
  428.9 12.6 copy-start.3
  428.9 12.6 copy-start.9
  428.9 12.6 copy-start.23
  468.2 12.7 copy-start.8
  488.4 18.7 %copy-start.43 = (f32[12]{0:T(128)S(1)}, f32[12]{0:T(128)}, u32[]{:S(2)}) copy-start(f32[12]{0:T(128)} %get-tuple-element.1173) | copy-start | bytes 148 | tf_op jit(solution)/shard_map/transpose(jvp())/while
  504.7 13.0 %copy-start.1 = (f32[2,256,128]{2,1,0:T(8,128)S(1)}, f32[2,256,128]{2,1,0:T(8,128)}, u32[]{:S(2)}) copy-start(f32[2,256,128]{2,1,0:T(8,128)} %get-tuple-element.1086) | copy-start | bytes 786436 | tf_op jit(solution)/shard_map/transpose(jvp())/while
  507.1 13.7 %copy-start.44 = (f32[12]{0:T(128)}, f32[12]{0:T(128)S(1)}, u32[]{:S(2)}) copy-start(f32[12]{0:T(128)S(1)} %fusion.230) | copy-start | bytes 148 | tf_op jit(solution)/shard_map/transpose(jvp())/while
  547.5 12.7 copy-start.8
  567.7 18.7 %copy-start.43 = (f32[12]{0:T(128)S(1)}, f32[12]{0:T(128)}, u32[]{:S(2)}) copy-start(f32[12]{0:T(128)} %get-tuple-element.1173) | copy-start | bytes 148 | tf_op jit(solution)/shard_map/transpose(jvp())/while
  584.0 13.0 %copy-start.1 = (f32[2,256,128]{2,1,0:T(8,128)S(1)}, f32[2,256,128]{2,1,0:T(8,128)}, u32[]{:S(2)}) copy-start(f32[2,256,128]{2,1,0:T(8,128)} %get-tuple-element.1086) | copy-start | bytes 786436 | tf_op jit(solution)/shard_map/transpose(jvp())/while
  586.4 13.7 %copy-start.44 = (f32[12]{0:T(128)}, f32[12]{0:T(128)S(1)}, u32[]{:S(2)}) copy-start(f32[12]{0:T(128)S(1)} %fusion.230) | copy-start | bytes 148 | tf_op jit(solution)/shard_map/transpose(jvp())/while
  626.8 12.7 copy-start.8
  646.9 18.7 %copy-start.43 = (f32[12]{0:T(128)S(1)}, f32[12]{0:T(128)}, u32[]{:S(2)}) copy-start(f32[12]{0:T(128)} %get-tuple-element.1173) | copy-start | bytes 148 | tf_op jit(solution)/shard_map/transpose(jvp())/while
  663.3 13.1 %copy-start.1 = (f32[2,256,128]{2,1,0:T(8,128)S(1)}, f32[2,256,128]{2,1,0:T(8,128)}, u32[]{:S(2)}) copy-start(f32[2,256,128]{2,1,0:T(8,128)} %get-tuple-element.1086) | copy-start | bytes 786436 | tf_op jit(solution)/shard_map/transpose(jvp())/while
  665.7 13.7 %copy-start.44 = (f32[12]{0:T(128)}, f32[12]{0:T(128)S(1)}, u32[]{:S(2)}) copy-start(f32[12]{0:T(128)S(1)} %fusion.230) | copy-start | bytes 148 | tf_op jit(solution)/shard_map/transpose(jvp())/while
  694.0 144.7 %reduce-scatter.17.cloned.1.call-start = ((), (), s32[]{:S(2)}) async-start(), calls=%async_computation.18 | async-start | bytes 417792
  712.9 16.6 %copy-start.35 = (f32[768]{0:T(1024)S(1)}, f32[768]{0:T(1024)}, u32[]{:S(2)}) copy-start(f32[768]{0:T(1024)} %copy-done.34) | copy-start | bytes 9220
  712.9 16.6 %copy-start.37 = (f32[768]{0:T(1024)S(1)}, f32[768]{0:T(1024)}, u32[]{:S(2)}) copy-start(f32[768]{0:T(1024)} %copy-done.36) | copy-start | bytes 9220
  712.9 16.6 %copy-start.39 = (f32[768]{0:T(1024)S(1)}, f32[768]{0:T(1024)}, u32[]{:S(2)}) copy-start(f32[768]{0:T(1024)} %get-tuple-element.805) | copy-start | bytes 9220
  712.9 16.6 %copy-start.41 = (f32[768]{0:T(1024)S(1)}, f32[768]{0:T(1024)}, u32[]{:S(2)}) copy-start(f32[768]{0:T(1024)} %get-tuple-element.806) | copy-start | bytes 9220
  744.7 12.7 copy-start.7
  756.6 115.3 %all-gather.18.cloned.1.call-start = ((), (), s32[]{:S(2)}) async-start(), calls=%async_computation.10 | async-start | bytes 3538944 | tf_op jit(solution)/shard_map/all_gather | solution.py:169
  757.3 249.1 %all-reduce.26.cloned.1.call-start = ((), (), s32[]{:S(2)}) async-start(), calls=%async_computation.12 | async-start | bytes 1572864 | tf_op jit(solution)/shard_map/psum | solution.py:247
  767.6 302.6 %all-gather.22.cloned.1.call-start = ((), (), s32[]{:S(2)}) async-start(), calls=%async_computation.15 | async-start | bytes 7151616 | tf_op jit(solution)/shard_map/all_gather | solution.py:170
  772.5 365.5 %reduce-scatter.11.cloned.1.call-start = ((), (), s32[]{:S(2)}) async-start(), calls=%async_computation.13 | async-start | bytes 2506752 | tf_op jit(solution)/shard_map/reduce_scatter | solution.py:245
  779.6 424.7 %reduce-scatter.15.cloned.1.call-start = ((), (), s32[]{:S(2)}) async-start(), calls=%async_computation.17 | async-start | bytes 2506752
  785.7 41.8 %all-to-all-start = ((bf16[2,1024,768]{1,2,0:T(8,128)(2,1)}), bf16[2,1024,768]{1,2,0:T(8,128)(2,1)}, u32[]{:S(2)}, u32[]{:S(2)}) async-start(bf16[2,1024,768]{1,2,0:T(8,128)(2,1)} %get-tuple-element.890), calls=%async_computation | async-start | bytes 6291456 | tf_op jit(solution)/shard_map/all_to_all | solution.py:167
  800.0 34.1 %copy-start.47 = (f32[768]{0:T(1024)S(1)}, f32[768]{0:T(1024)}, u32[]{:S(2)}) copy-start(f32[768]{0:T(1024)} %get-tuple-element.864) | copy-start | bytes 9220
  827.5 180.3 %all-to-all-start.1 = ((bf16[2,1024,1548]{1,2,0:T(8,128)(2,1)}), bf16[2,1024,1548]{1,2,0:T(8,128)(2,1)}, u32[]{:S(2)}, u32[]{:S(2)}) async-start(bf16[2,1024,1548]{1,2,0:T(8,128)(2,1)} %pad_maximum_fusion), calls=%async_computation.1 | async-start | bytes 12713984 | tf_op jit(solution)/shard_map/all_to_all | solution.py:203
  834.1 37.8 %copy-start.5 = (bf16[1,1024,768]{2,1,0:T(8,128)(2,1)S(1)}, bf16[1,1024,768]{2,1,0:T(8,128)(2,1)}, u32[]{:S(2)}) copy-start(bf16[1,1024,768]{2,1,0:T(8,128)(2,1)} %param.20) | copy-start | bytes 4718596
  834.1 437.0 %reduce-scatter.13.cloned.1.call-start = ((), (), s32[]{:S(2)}) async-start(), calls=%async_computation.16 | async-start | bytes 2506752
  1084.8 47.8 %copy-start.12 = (bf16[1,1024,768]{2,1,0:T(8,128)(2,1)S(1)}, bf16[1,1024,768]{2,1,0:T(8,128)(2,1)}, u32[]{:S(2)}) copy-start(bf16[1,1024,768]{2,1,0:T(8,128)(2,1)} %param.35) | copy-start | bytes 4718596
  1084.8 47.8 %copy-start.46 = (f32[1024]{0:T(1024)S(1)}, f32[1024]{0:T(1024)}, u32[]{:S(2)}) copy-start(f32[1024]{0:T(1024)} %get-tuple-element.905) | copy-start | bytes 12292
  (79 other events, 599.6 us)
Sparse Core Ops, SparseCore 0:
  10.4 41.0 all-gather.13
  53.8 37.2 all-gather.11
  93.2 43.8 all-gather.9
  139.2 38.3 all-gather.15
  179.0 43.8 all-gather.19
  694.2 63.1 all-reduce.27
  761.8 55.5 reduce-scatter.16
  818.9 52.9 all-gather.17
  877.1 129.3 all-reduce.25
  1007.9 62.1 all-gather.21
  1075.0 63.0 reduce-scatter.10
  1142.2 61.9 reduce-scatter.14
  1209.0 61.9 reduce-scatter.12
where the time goes:
time: 1290 us; the launch traced here: 1280 us
  waiting for transfers between devices  442 us (34%)
  matrix products  295 us (23%)
  local copies, waits for them, and re-layouts  236 us (18%)
  other arithmetic  183 us (14%)
  blocking collectives  93.1 us (7%)
  between operations  14.9 us (1%)
    unnamed x16, waiting for transfers between devices  136 us
    psum x1, waiting for transfers between devices, local(): lax.psum((small[0], small[1], small[2], small[3], small[4], small[5], sma...  128 us
    dot_general x12, matrix products, advance(): jnp.einsum('shqk,skhp->sqhp', mixing, value_blk, precision=exact_precision)  112 us
    all_gather x1, waiting for transfers between devices, local(): lax.all_gather(leading_part, 'tensor', axis=1, tiled=True)  55.2 us
    dot_general x16, matrix products, advance(): jnp.einsum('sqn,shpn->sqhp', read_blk, state, precision=exact_precision)  47.4 us
    dot_general x12, matrix products, advance(): jnp.einsum('skn,skhp->shpn', write_blk, value_blk * remain[..., None], pr...  45.5 us
    another operation x38, other arithmetic  41.5 us
    psum x1, blocking collectives, local(): lax.psum((small[0], small[1], small[2], small[3], small[4], small[5], sma...  41.2 us
  transfers between devices with their start and end apart: 15, of which 9 were waited for; matrix products, arithmetic and copies ran while one was open for 26% of the time, Pallas kernels for 0%

commit v1 on v0

v1 whole, which is shorter than its diff:
```python
import functools

import jax
import jax.numpy as jnp
from jax import lax
from jax.experimental import pallas as pl
from jax.experimental.pallas import tpu as pltpu
from jax.sharding import PartitionSpec as P

BLOCK = 256
HALVES = 2
PAD = 128
EPS = 1e-05
NEG = -1e30
F32 = jnp.float32
BF16 = jnp.bfloat16
VMEM_BYTES = 56 * 1024 * 1024


def dot(a, b):
    return jnp.dot(a, b, preferred_element_type=F32)


def dot_nt(a, b):
    return lax.dot_general(a, b, (((1,), (1,)), ((), ())), preferred_element_type=F32)


def dot_tn(a, b):
    return lax.dot_general(a, b, (((0,), (0,)), ((), ())), preferred_element_type=F32)


def split3(v):
    high = v.astype(BF16)
    rest = v - high.astype(F32)
    mid = rest.astype(BF16)
    low = (rest - mid.astype(F32)).astype(BF16)
    return high, mid, low


def dot_exact(mask, v):
    high, mid, low = split3(v)
    return dot(mask, high) + dot(mask, mid) + dot(mask, low)


def sigmoid(v):
    return 1.0 / (1.0 + jnp.exp(-v))


def spread(cols, pair, lane_low):
    rows = cols.shape[0]
    left = jnp.broadcast_to(cols[:, 2 * pair : 2 * pair + 1], (rows, 128))
    right = jnp.broadcast_to(cols[:, 2 * pair + 1 : 2 * pair + 2], (rows, 128))
    return jnp.where(lane_low, left, right)


def conv_taps(buf, taps_ref, shift_ref, first, rows):
    total = shift_ref[...] + taps_ref[0:1, :] * buf[pl.ds(first, rows), :]
    for j in range(1, 4):
        total = total + taps_ref[j : j + 1, :] * buf[pl.ds(first + j, rows), :]
    return total


def maps_kernel(
    x_ref, gain_ref, ws_ref, wt0_ref, wt1_ref, taps_ref, shift_ref, tshift_ref, rate_ref,
    normed_ref, statein_ref, statec_ref, maps_ref, mapst_ref, cumc_ref, dtc_ref, sgc_ref, cumr_ref,
    buf,
):
    step = pl.program_id(0)

    @pl.when(step == 0)
    def _():
        buf[pl.ds(0, 8), :] = jnp.zeros((8, buf.shape[1]), F32)

    x = x_ref[0].astype(F32)
    inv = lax.rsqrt(jnp.mean(x * x, axis=-1, keepdims=True) + EPS)
    normed = (x * inv * gain_ref[...]).astype(BF16)
    normed_ref[...] = normed
    state_in = dot(normed, ws_ref[0])
    statein_ref[...] = state_in
    buf[pl.ds(8, BLOCK), :] = state_in
    c = conv_taps(buf, taps_ref, shift_ref, 5, BLOCK)
    buf[pl.ds(0, 8), :] = buf[pl.ds(BLOCK, 8), :]
    statec_ref[...] = c
    maps = c * sigmoid(c)
    maps_ref[...] = maps.astype(BF16)
    mapst_ref[...] = maps.T.astype(BF16)
    row = lax.broadcasted_iota(jnp.int32, (BLOCK, BLOCK), 0)
    col = lax.broadcasted_iota(jnp.int32, (BLOCK, BLOCK), 1)
    lower = jnp.where(row >= col, 1.0, 0.0).astype(BF16)
    for half, wt_ref in enumerate((wt0_ref, wt1_ref)):
        raw = dot(normed, wt_ref[0]) + tshift_ref[half : half + 1, :]
        soft = jnp.exp(-jnp.abs(raw))
        dt = jnp.maximum(raw, 0.0) + jnp.log1p(soft)
        dtc_ref[half] = dt
        sgc_ref[half] = jnp.where(raw >= 0, 1.0, soft) / (1.0 + soft)
        cum = dot_exact(lower, dt * rate_ref[half : half + 1, :])
        cumc_ref[half] = cum
        cumr_ref[half] = cum.T[0:16, :]


def forward_kernel(
    normed_ref, wv_ref, taps_ref, shift_ref, skip_ref, maps_ref, mapst_ref, cumc_ref, dtc_ref, cumr_ref,
    vin_ref, c_ref, y_ref, state_ref,
    buf, state,
):
    step = pl.program_id(1)
    width = buf.shape[1]
    n = state.shape[0]

    @pl.when(step == 0)
    def _():
        buf[pl.ds(0, 8), :] = jnp.zeros((8, width), F32)
        state[...] = jnp.zeros(state.shape, F32)

    value_in = dot(normed_ref[...], wv_ref[0])
    vin_ref[0] = value_in.astype(BF16)
    buf[pl.ds(8, BLOCK), :] = value_in
    c = conv_taps(buf, taps_ref, shift_ref, 5, BLOCK)
    buf[pl.ds(0, 8), :] = buf[pl.ds(BLOCK, 8), :]
    c_ref[0] = c
    state_ref[0, 0] = state[...]
    write = maps_ref[:, 0:n]
    read = maps_ref[:, n : 2 * n]
    write_t = mapst_ref[0:n, :]
    grams = dot_nt(read, write)
    carried = dot(read, state[...].astype(BF16))
    cumc = cumc_ref[0]
    dtc = dtc_ref[0]
    ecum = jnp.exp(cumc)
    rem = jnp.exp(cumc[BLOCK - 1 : BLOCK, :] - cumc) * dtc
    lane_low = lax.broadcasted_iota(jnp.int32, (BLOCK, 128), 1) < 64
    hb = BLOCK // 2
    tri = lax.broadcasted_iota(jnp.int32, (hb, hb), 0) >= lax.broadcasted_iota(jnp.int32, (hb, hb), 1)
    zeros = jnp.zeros((hb, hb), BF16)
    g00 = grams[0:hb, 0:hb]
    g10 = grams[hb:, 0:hb]
    g11 = grams[hb:, hb:]
    for pair in range(width // 128):
        lanes = slice(pair * 128, pair * 128 + 128)
        cp = c[:, lanes]
        v = cp * sigmoid(cp)
        vdt = (v * spread(dtc, pair, lane_low)).astype(BF16)
        outs = []
        for j in range(2):
            h = 2 * pair + j
            cq = jnp.broadcast_to(cumc[:, h : h + 1], (BLOCK, hb))
            ck = cumr_ref[0, h : h + 1, :]
            d00 = jnp.exp(jnp.where(tri, cq[0:hb] - ck[:, 0:hb], NEG))
            d10 = jnp.exp(cq[hb:] - ck[:, 0:hb])
            d11 = jnp.exp(jnp.where(tri, cq[hb:] - ck[:, hb:], NEG))
            top = jnp.concatenate([(g00 * d00).astype(BF16), zeros], axis=1)
            bot = jnp.concatenate([(g10 * d10).astype(BF16), (g11 * d11).astype(BF16)], axis=1)
            outs.append(dot(jnp.concatenate([top, bot], axis=0), vdt))
        ec = spread(ecum, pair, lane_low)
        y = jnp.where(lane_low, outs[0], outs[1]) + ec * carried[:, lanes] + skip_ref[:, lanes] * v
        y_ref[0, :, lanes] = y
        vrem = (v * spread(rem, pair, lane_low)).astype(BF16)
        state[:, lanes] = state[:, lanes] * ec[BLOCK - 1 : BLOCK, :] + dot(write_t, vrem)


def gated_kernel(
    x_ref, cot_ref, normed_ref, y_ref, wg_ref, wo_ref, gain_ref,
    result_ref, dy_ref, dgate_ref, outg_ref, gateg_ref, gaing_ref,
):
    step = pl.program_id(0)

    @pl.when(step == 0)
    def _():
        outg_ref[...] = jnp.zeros(outg_ref.shape, F32)
        gateg_ref[...] = jnp.zeros(gateg_ref.shape, F32)
        gaing_ref[...] = jnp.zeros(gaing_ref.shape, F32)

    width = wg_ref.shape[2]
    normed = normed_ref[...]
    cot = cot_ref[0]
    gates, mixes = [], []
    squares = 0.0
    for half in range(HALVES):
        gate = dot(normed, wg_ref[half])
        mixed = y_ref[half] * (gate * sigmoid(gate))
        squares = squares + jnp.sum(mixed * mixed, axis=-1, keepdims=True)
        gates.append(gate)
        mixes.append(mixed)
    rms = lax.rsqrt(squares / (HALVES * width) + EPS)
    total = x_ref[0].astype(F32)
    inner = 0.0
    scaled = []
    for half in range(HALVES):
        gain = gain_ref[half : half + 1, :]
        gated = (mixes[half] * rms * gain).astype(BF16)
        total = total + dot_nt(gated, wo_ref[half])
        outg_ref[half] += dot_tn(cot, gated)
        grad = dot(cot, wo_ref[half])
        gaing_ref[half : half + 1, :] += jnp.sum(grad * mixes[half] * rms, axis=0, keepdims=True)
        grad = grad * gain
        inner = inner + jnp.sum(grad * mixes[half], axis=-1, keepdims=True)
        scaled.append(grad)
    result_ref[0] = total.astype(BF16)
    factor = rms * rms * rms * (inner / (HALVES * width))
    for half in range(HALVES):
        grad_mixed = rms * scaled[half] - mixes[half] * factor
        gate = gates[half]
        sg = sigmoid(gate)
        dy_ref[half] = (grad_mixed * (gate * sg)).astype(BF16)
        dgate = (grad_mixed * y_ref[half] * (sg * (1.0 + gate * (1.0 - sg)))).astype(BF16)
        dgate_ref[half] = dgate
        gateg_ref[half] += dot_tn(normed, dgate)


def backward_kernel(
    c_ref, vin_ref, dy_ref, state_ref, maps_ref, mapst_ref, cumc_ref, dtc_ref, sgc_ref, cumr_ref,
    taps_ref, skip_ref, rate_ref,
    dvin_ref, dmaps_ref, dstep_ref, tapsg_ref, headg_ref,
    buf, dstate, dgt, uacc, vacc,
):
    step = pl.program_id(1)
    width = buf.shape[1]
    n = dstate.shape[0]
    hb = BLOCK // 2

    @pl.when(step == 0)
    def _():
        buf[pl.ds(BLOCK, 8), :] = jnp.zeros((8, width), F32)
        dstate[...] = jnp.zeros(dstate.shape, F32)
        tapsg_ref[...] = jnp.zeros(tapsg_ref.shape, F32)
        headg_ref[...] = jnp.zeros(headg_ref.shape, F32)

    write = maps_ref[:, 0:n]
    read = maps_ref[:, n : 2 * n]
    read_t = mapst_ref[n : 2 * n, :]
    gt = dot_nt(write, read)
    state = state_ref[0, 0]
    ds = dstate[...]
    ds_b = ds.astype(BF16)
    carried = dot(read, state.astype(BF16))
    wds = dot(write, ds_b)
    cumc = cumc_ref[0]
    dtc = dtc_ref[0]
    ecum = jnp.exp(cumc)
    last = jnp.exp(cumc[BLOCK - 1 : BLOCK, :] - cumc)
    rem = last * dtc
    lane = lax.broadcasted_iota(jnp.int32, (BLOCK, 128), 1)
    lane_low = lane < 64
    sub = lax.broadcasted_iota(jnp.int32, (16, BLOCK), 0)
    tri = lax.broadcasted_iota(jnp.int32, (hb, hb), 1) >= lax.broadcasted_iota(jnp.int32, (hb, hb), 0)
    zeros = jnp.zeros((hb, hb), BF16)
    g00 = gt[0:hb, 0:hb]
    g01 = gt[0:hb, hb:]
    g11 = gt[hb:, hb:]
    dgt[...] = jnp.zeros(dgt.shape, F32)
    to_k = jnp.zeros((BLOCK, 128), F32)
    to_q = jnp.zeros((16, BLOCK), F32)
    for pair in range(width // 128):
        lanes = slice(pair * 128, pair * 128 + 128)
        cp = c_ref[0, :, lanes]
        v = cp * sigmoid(cp)
        vacc[:, lanes] = v
        dt_s = spread(dtc, pair, lane_low)
        vdt = (v * dt_s).astype(BF16)
        dyp = dy_ref[0, :, lanes]
        us = []
        for j in range(2):
            h = 2 * pair + j
            ck = jnp.broadcast_to(cumc[:, h : h + 1], (BLOCK, hb))
            cq = cumr_ref[0, h : h + 1, :]
            d00 = jnp.exp(jnp.where(tri, cq[:, 0:hb] - ck[0:hb], NEG))
            d01 = jnp.exp(cq[:, hb:] - ck[0:hb])
            d11 = jnp.exp(jnp.where(tri, cq[:, hb:] - ck[hb:], NEG))
            mine = jnp.where(lane_low if j == 0 else jnp.logical_not(lane_low), dyp, jnp.zeros_like(dyp))
            qt = dot_nt(vdt, mine)
            e00 = d00 * qt[0:hb, 0:hb]
            e01 = d01 * qt[0:hb, hb:]
            e11 = d11 * qt[hb:, hb:]
            dgt[0:hb, 0:hb] += e00
            dgt[0:hb, hb:] += e01
            dgt[hb:, hb:] += e11
            a = jnp.concatenate(
                [
                    jnp.concatenate([(g00 * d00).astype(BF16), (g01 * d01).astype(BF16)], axis=1),
                    jnp.concatenate([zeros, (g11 * d11).astype(BF16)], axis=1),
                ],
                axis=0,
            )
            z = jnp.concatenate(
                [
                    jnp.concatenate([(g00 * e00).astype(BF16), (g01 * e01).astype(BF16)], axis=1),
                    jnp.concatenate([zeros, (g11 * e11).astype(BF16)], axis=1),
                ],
                axis=0,
            )
            us.append(dot(a, dyp))
            to_k = to_k + dot(z, jnp.where(lane == h, 1.0, 0.0).astype(BF16))
            to_q = to_q + dot(jnp.where(sub == h, 1.0, 0.0).astype(BF16), z)
        uacc[:, lanes] = jnp.where(lane_low, us[0], us[1])
        ec = spread(ecum, pair, lane_low)
        dye = (dyp.astype(F32) * ec).astype(BF16)
        u = uacc[:, lanes]
        dv = dt_s * u + skip_ref[:, lanes] * dyp.astype(F32) + spread(rem, pair, lane_low) * wds[:, lanes]
        sg = sigmoid(cp)
        buf[0:BLOCK, lanes] = dv * (sg * (1.0 + cp * (1.0 - sg)))
        dstate[:, lanes] = ds[:, lanes] * ec[BLOCK - 1 : BLOCK, :] + dot(read_t, dye)
        vrem = (v * spread(rem, pair, lane_low)).astype(BF16)
        dmw = dot_nt(vrem, ds_b[:, lanes])
        dmr = dot_nt(dye, state[:, lanes].astype(BF16))
        if pair == 0:
            dmaps_w, dmaps_r = dmw, dmr
        else:
            dmaps_w, dmaps_r = dmaps_w + dmw, dmaps_r + dmr
    dg_b = dgt[...].astype(BF16)
    dmaps_ref[0, :, 0:n] = dmaps_w + dot(dg_b, read)
    dmaps_ref[0, :, n : 2 * n] = dmaps_r + dot_tn(dg_b, write)

    row = lax.broadcasted_iota(jnp.int32, (width, 128), 0)
    col = lax.broadcasted_iota(jnp.int32, (width, 128), 1)
    pick = jnp.where(row // 64 == col, 1.0, 0.0).astype(BF16)

    def per_head(values):
        high = values.astype(BF16)
        low = (values - high.astype(F32)).astype(BF16)
        return dot(high, pick) + dot(low, pick)

    v = vacc[...]
    dy = dy_ref[0].astype(F32)
    v_u = per_head(v * uacc[...])
    v_wds = per_head(v * wds)
    dy_c = per_head(dy * carried)
    skip_sum = jnp.sum(dy * v, axis=0, keepdims=True)
    ss = per_head(jnp.broadcast_to(jnp.sum(ds * state, axis=0, keepdims=True), (8, width)))
    sent = rem * v_wds
    d_last = ecum[BLOCK - 1 : BLOCK, :] * ss[0:1, :] + jnp.sum(sent, axis=0, keepdims=True)
    dcum = jnp.concatenate([to_q, jnp.zeros((112, BLOCK), F32)], axis=0).T - to_k + ecum * dy_c - sent
    token = lax.broadcasted_iota(jnp.int32, (BLOCK, 128), 0)
    dcum = dcum + jnp.where(token == BLOCK - 1, d_last, 0.0)
    row = lax.broadcasted_iota(jnp.int32, (BLOCK, BLOCK), 0)
    col = lax.broadcasted_iota(jnp.int32, (BLOCK, BLOCK), 1)
    upper = jnp.where(row <= col, 1.0, 0.0).astype(BF16)
    dlog = dot_exact(upper, dcum)
    rate = rate_ref[0]
    ddt = v_u + last * v_wds + dlog * rate
    draw = ddt * sgc_ref[0]
    dstep_ref[0] = draw.astype(BF16)
    headg_ref[0, 0:1, :] += jnp.sum(draw, axis=0, keepdims=True)
    headg_ref[0, 1:2, :] += jnp.sum(dlog * dtc, axis=0, keepdims=True) * rate
    headg_ref[0, 2:3, :] += per_head(jnp.broadcast_to(skip_sum, (8, width)))[0:1, :]

    vin = vin_ref[0].astype(F32)
    total = jnp.zeros((BLOCK, width), F32)
    for j in range(4):
        shifted = buf[pl.ds(3 - j, BLOCK), :]
        total = total + taps_ref[j : j + 1, :] * shifted
        tapsg_ref[0, j : j + 1, :] += jnp.sum(shifted * vin, axis=0, keepdims=True)
    tapsg_ref[0, 4:5, :] += jnp.sum(buf[0:BLOCK, :], axis=0, keepdims=True)
    dvin_ref[0] = total.astype(BF16)
    buf[pl.ds(BLOCK, 8), :] = buf[pl.ds(0, 8), :]


def state_kernel(dmaps_ref, statein_ref, statec_ref, taps_ref, dstate_ref, tapsg_ref, buf):
    length, width = statein_ref.shape
    c = statec_ref[...]
    sg = sigmoid(c)
    dc = (dmaps_ref[0] + dmaps_ref[1]) * (sg * (1.0 + c * (1.0 - sg)))
    buf[0:length, :] = dc
    buf[pl.ds(length, 8), :] = jnp.zeros((8, width), F32)
    state_in = statein_ref[...]
    total = jnp.zeros((length, width), F32)
    tapsg_ref[...] = jnp.zeros(tapsg_ref.shape, F32)
    for j in range(4):
        shifted = buf[pl.ds(3 - j, length), :]
        total = total + taps_ref[j : j + 1, :] * shifted
        tapsg_ref[j : j + 1, :] = jnp.sum(shifted * state_in, axis=0, keepdims=True)
    tapsg_ref[4:5, :] = jnp.sum(dc, axis=0, keepdims=True)
    dstate_ref[...] = total.astype(BF16)


def input_kernel(
    x_ref, cot_ref, gain_ref, dgate_ref, dvin_ref, dstate_ref, dstep_ref, wg_ref, wv_ref, ws_ref, wt0_ref, wt1_ref,
    grad_ref, gaing_ref,
):
    step = pl.program_id(0)

    @pl.when(step == 0)
    def _():
        gaing_ref[...] = jnp.zeros(gaing_ref.shape, F32)

    total = dot_nt(dstate_ref[...], ws_ref[0])
    for half, wt_ref in enumerate((wt0_ref, wt1_ref)):
        total = total + dot_nt(dgate_ref[half], wg_ref[half])
        total = total + dot_nt(dvin_ref[half], wv_ref[half])
        total = total + dot_nt(dstep_ref[half], wt_ref[0])
    x = x_ref[0].astype(F32)
    inv = lax.rsqrt(jnp.mean(x * x, axis=-1, keepdims=True) + EPS)
    gaing_ref[0:1, :] += jnp.sum(total * x * inv, axis=0, keepdims=True)
    scaled = total * gain_ref[...]
    inner = jnp.mean(scaled * x, axis=-1, keepdims=True)
    grad_ref[0] = cot_ref[0].astype(F32) + inv * scaled - x * (inv * inv * inv * inner)


def call(body, grid, in_specs, out_specs, out_shape, scratch=(), flops=0):
    return pl.pallas_call(
        body,
        grid=grid,
        in_specs=in_specs,
        out_specs=out_specs,
        out_shape=out_shape,
        scratch_shapes=list(scratch),
        compiler_params=pltpu.CompilerParams(
            vmem_limit_bytes=VMEM_BYTES, dimension_semantics=("arbitrary",) * len(grid)
        ),
        cost_estimate=pl.CostEstimate(flops=flops, bytes_accessed=10_000_000, transcendentals=0),
    )


def shape(dims, dtype=F32):
    return jax.ShapeDtypeStruct(dims, dtype)


def fixed(dims, *index):
    return pl.BlockSpec(dims, lambda *_: index)


def local(
    inputs,
    prenorm,
    gate_weight,
    value_weight,
    state_weight,
    step_weight,
    value_conv,
    value_shift,
    state_conv,
    state_shift,
    step_shift,
    decay_log,
    skip_scale,
    gated_gain,
    output_matrix,
    cotangent,
):
    both = ("tensor", "dp")
    place = lax.axis_index("tensor")
    length, width = inputs.shape[1:]
    rows, half_width = gate_weight.shape
    heads = step_weight.shape[1]
    n = state_weight.shape[1] // 2
    blocks = length // BLOCK
    head_width = half_width // heads

    def lanes_of(v):
        return jnp.pad(v, ((0, 0), (0, PAD - v.shape[1])))

    pack = jnp.concatenate([value_weight, state_weight, lanes_of(step_weight)], axis=1)
    first = lax.all_gather(pack, both, axis=0, tiled=True).reshape(HALVES, width, pack.shape[1])
    pack = jnp.concatenate([gate_weight, output_matrix.T], axis=1)
    second = lax.all_gather(pack, both, axis=0, tiled=True).reshape(HALVES, width, pack.shape[1])
    small = jnp.concatenate(
        [
            value_conv.reshape(-1), value_shift, jnp.repeat(skip_scale, head_width), gated_gain,
            lanes_of(step_shift[None]).reshape(-1), lanes_of(-jnp.exp(decay_log)[None]).reshape(-1),
        ]
    )
    small = lax.all_gather(small, "tensor", axis=0)
    w = half_width
    value_taps = jnp.moveaxis(small[:, : 4 * w].reshape(HALVES, 4, w), 0, 1).reshape(4, HALVES * w)
    value_bias = small[:, 4 * w : 5 * w].reshape(1, HALVES * w)
    skip = small[:, 5 * w : 6 * w].reshape(1, HALVES * w)
    gain = small[:, 6 * w : 7 * w]
    step_bias = small[:, 7 * w : 7 * w + PAD]
    rate = small[:, 7 * w + PAD :]

    ws_spec = fixed((1, width, 2 * n), 0, 0, w // (2 * n))
    wt_specs = [fixed((1, width, PAD), half, 0, (w + 2 * n) // PAD) for half in range(HALVES)]
    row_block = lambda dims, dtype=None: pl.BlockSpec(dims, lambda b: (b, 0))
    tokens = pl.BlockSpec((1, BLOCK, width), lambda b: (0, b, 0))
    halves = lambda last: pl.BlockSpec((HALVES, BLOCK, last), lambda b: (0, b, 0))

    normed, state_in, state_c, maps, maps_t, cumc, dtc, sgc, cumr = call(
        maps_kernel,
        (blocks,),
        [tokens, fixed((1, width), 0, 0), ws_spec, *wt_specs, fixed((4, 2 * n), 0, 0), fixed((1, 2 * n), 0, 0),
         fixed((HALVES, PAD), 0, 0), fixed((HALVES, PAD), 0, 0)],
        [row_block((BLOCK, width)), row_block((BLOCK, 2 * n)), row_block((BLOCK, 2 * n)), row_block((BLOCK, 2 * n)),
         pl.BlockSpec((2 * n, BLOCK), lambda b: (0, b)), halves(PAD), halves(PAD), halves(PAD),
         pl.BlockSpec((HALVES, 16, BLOCK), lambda b: (0, 0, b))],
        [shape((length, width), BF16), shape((length, 2 * n)), shape((length, 2 * n)), shape((length, 2 * n), BF16),
         shape((2 * n, length), BF16), shape((HALVES, length, PAD)), shape((HALVES, length, PAD)),
         shape((HALVES, length, PAD)), shape((HALVES, 16, length))],
        [pltpu.VMEM((BLOCK + 8, 2 * n), F32)],
        flops=2 * length * width * 512,
    )(inputs, prenorm[None], first, first, first, state_conv, state_shift[None], step_bias, rate)

    def fwd(dims):
        return pl.BlockSpec(dims, lambda h, b: (h, b, 0))

    def channel(dims):
        return pl.BlockSpec(dims, lambda h, b: (0, h))

    value_in, value_c, mixed, states = call(
        forward_kernel,
        (HALVES, blocks),
        [pl.BlockSpec((BLOCK, width), lambda h, b: (b, 0)), pl.BlockSpec((1, width, w), lambda h, b: (h, 0, 0)),
         channel((4, w)), channel((1, w)), channel((1, w)),
         pl.BlockSpec((BLOCK, 2 * n), lambda h, b: (b, 0)), pl.BlockSpec((2 * n, BLOCK), lambda h, b: (0, b)),
         fwd((1, BLOCK, PAD)), fwd((1, BLOCK, PAD)), pl.BlockSpec((1, 16, BLOCK), lambda h, b: (h, 0, b))],
        [fwd((1, BLOCK, w)), fwd((1, BLOCK, w)), fwd((1, BLOCK, w)),
         pl.BlockSpec((1, 1, n, w), lambda h, b: (h, b, 0, 0))],
        [shape((HALVES, length, w), BF16), shape((HALVES, length, w)), shape((HALVES, length, w)),
         shape((HALVES, blocks, n, w))],
        [pltpu.VMEM((BLOCK + 8, w), F32), pltpu.VMEM((n, w), F32)],
        flops=20_000_000_000,
    )(normed, first, value_taps, value_bias, skip, maps, maps_t, cumc, dtc, cumr)

    wg_spec = fixed((HALVES, width, w), 0, 0, 0)
    result, dy, dgate, out_partial, gate_partial, gain_partial = call(
        gated_kernel,
        (blocks,),
        [tokens, tokens, row_block((BLOCK, width)), halves(w), wg_spec, fixed((HALVES, width, w), 0, 0, 1),
         fixed((HALVES, w), 0, 0)],
        [tokens, halves(w), halves(w), fixed((HALVES, width, w), 0, 0, 0), fixed((HALVES, width, w), 0, 0, 0),
         fixed((HALVES, w), 0, 0)],
        [shape(inputs.shape, BF16), shape((HALVES, length, w), BF16), shape((HALVES, length, w), BF16),
         shape((HALVES, width, w)), shape((HALVES, width, w)), shape((HALVES, w))],
        flops=20_000_000_000,
    )(inputs, cotangent, normed, mixed, second, second, gain)

    back = lambda dims: pl.BlockSpec(dims, lambda h, b: (h, blocks - 1 - b, 0))
    dvalue, dmaps, dstep, taps_partial, head_partial = call(
        backward_kernel,
        (HALVES, blocks),
        [back((1, BLOCK, w)), back((1, BLOCK, w)), back((1, BLOCK, w)),
         pl.BlockSpec((1, 1, n, w), lambda h, b: (h, blocks - 1 - b, 0, 0)),
         pl.BlockSpec((BLOCK, 2 * n), lambda h, b: (blocks - 1 - b, 0)),
         pl.BlockSpec((2 * n, BLOCK), lambda h, b: (0, blocks - 1 - b)),
         back((1, BLOCK, PAD)), back((1, BLOCK, PAD)), back((1, BLOCK, PAD)),
         pl.BlockSpec((1, 16, BLOCK), lambda h, b: (h, 0, blocks - 1 - b)),
         channel((4, w)), channel((1, w)), pl.BlockSpec((1, 1, PAD), lambda h, b: (h, 0, 0))],
        [back((1, BLOCK, w)), back((1, BLOCK, 2 * n)), back((1, BLOCK, PAD)),
         pl.BlockSpec((1, 8, w), lambda h, b: (h, 0, 0)), pl.BlockSpec((1, 8, PAD), lambda h, b: (h, 0, 0))],
        [shape((HALVES, length, w), BF16), shape((HALVES, length, 2 * n)), shape((HALVES, length, PAD), BF16),
         shape((HALVES, 8, w)), shape((HALVES, 8, PAD))],
        [pltpu.VMEM((BLOCK + 8, w), F32), pltpu.VMEM((n, w), F32), pltpu.VMEM((BLOCK, BLOCK), F32),
         pltpu.VMEM((BLOCK, w), F32), pltpu.VMEM((BLOCK, w), F32)],
        flops=40_000_000_000,
    )(value_c, value_in, dy, states, maps, maps_t, cumc, dtc, sgc, cumr, value_taps, skip, rate[:, None, :])

    dstate, state_taps = call(
        state_kernel,
        (1,),
        [fixed((HALVES, length, 2 * n), 0, 0, 0), fixed((length, 2 * n), 0, 0), fixed((length, 2 * n), 0, 0),
         fixed((4, 2 * n), 0, 0)],
        [fixed((length, 2 * n), 0, 0), fixed((8, 2 * n), 0, 0)],
        [shape((length, 2 * n), BF16), shape((8, 2 * n))],
        [pltpu.VMEM((length + 8, 2 * n), F32)],
        flops=1_000_000_000,
    )(dmaps, state_in, state_c, state_conv)

    input_grad, prenorm_partial = call(
        input_kernel,
        (blocks,),
        [tokens, tokens, fixed((1, width), 0, 0), halves(w), halves(w), row_block((BLOCK, 2 * n)), halves(PAD),
         wg_spec, wg_spec, ws_spec, *wt_specs],
        [tokens, fixed((8, width), 0, 0)],
        [shape(inputs.shape), shape((8, width))],
        flops=6_000_000_000,
    )(inputs, cotangent, prenorm[None], dgate, dvalue, dstate, dstep, second, first, first, first, first)

    value_partial = jnp.einsum("tk,htf->hkf", normed, dvalue, preferred_element_type=F32)
    state_partial = jnp.einsum("tk,tf->kf", normed, dstate, preferred_element_type=F32)
    step_partial = jnp.einsum("tk,htf->hkf", normed, dstep, preferred_element_type=F32)
    late = jnp.concatenate(
        [value_partial, jnp.broadcast_to(state_partial[None], (HALVES,) + state_partial.shape), step_partial], axis=2
    )
    early = jnp.concatenate([gate_partial, out_partial], axis=2)
    late = lax.psum_scatter(late.reshape(HALVES * width, -1), both, scatter_dimension=0, tiled=True)
    early = lax.psum_scatter(early.reshape(HALVES * width, -1), both, scatter_dimension=0, tiled=True)
    smalls = lax.psum(
        (taps_partial, head_partial, gain_partial, state_taps, prenorm_partial), both
    )
    taps_sum, head_sum, gain_sum, state_taps, prenorm_sum = smalls
    pick = lambda v: lax.dynamic_index_in_dim(v, place, 0, keepdims=False)
    taps_sum, head_sum, gain_sum = pick(taps_sum), pick(head_sum), pick(gain_sum)
    return (
        result,
        input_grad,
        prenorm_sum[0],
        early[:, :w],
        late[:, :w],
        late[:, w : w + 2 * n],
        late[:, w + 2 * n : w + 2 * n + heads],
        taps_sum[0:4],
        taps_sum[4],
        state_taps[0:4],
        state_taps[4],
        head_sum[0, :heads],
        head_sum[1, :heads],
        head_sum[2, :heads],
        gain_sum,
        early[:, w:].T,
    )


def solution(mesh):
    in_specs = (
        P(("dp", "tensor"), None, None),
        P(),
        P("dp", "tensor"),
        P("dp", "tensor"),
        P("dp", None),
        P("dp", "tensor"),
        P(None, "tensor"),
        P("tensor"),
        P(),
        P(),
        P("tensor"),
        P("tensor"),
        P("tensor"),
        P("tensor"),
        P("tensor", "dp"),
        P(("dp", "tensor"), None, None),
    )
    out_specs = (
        P(("dp", "tensor"), None, None),
        P(("dp", "tensor"), None, None),
        P(),
        P("dp", "tensor"),
        P("dp", "tensor"),
        P("dp", None),
        P("dp", "tensor"),
        P(None, "tensor"),
        P("tensor"),
        P(),
        P(),
        P("tensor"),
        P("tensor"),
        P("tensor"),
        P("tensor"),
        P("tensor", "dp"),
    )
    return jax.shard_map(local, mesh=mesh, in_specs=in_specs, out_specs=out_specs, check_vma=False)
```

time: 1290 us -> 640 us (0.50)
  matrix products: 295 us -> 9.1 us
  local copies, waits for them, and re-layouts: 236 us -> 30.8 us
  other arithmetic: 183 us -> 17.2 us
  Pallas kernels: 0 us -> 125 us
  blocking collectives: 93.1 us -> 5.4 us
    dot_general x64 -> x3, matrix products: 295 us -> 9.1 us  [the longest x1 6.78 us: local(): jnp.einsum('tk,htf->hkf', normed, dvalue, preferred_element_type=F32)]
    reduce_scatter x1 -> x2, waiting for transfers between devices: 1.85 us -> 255 us  [the longest x1 137 us: local(): lax.psum_scatter(early.reshape(HALVES * width, -1), both, scatter_dimensi...]
    unnamed x16 -> x5, waiting for transfers between devices: 136 us -> 0.08 us
    pallas_call x0 -> x6, Pallas kernels: none -> 125 us  [the longest x1 49.1 us: local(): call(backward_kernel, (HALVES, blocks), [back((1, BLOCK, w)), back((1, BL...]
    all_gather x7 -> x2, waiting for transfers between devices: 148 us -> 81.9 us  [local(): lax.all_gather(pack, both, axis=0, tiled=True)]
    reduce_sum x15 -> x0, other arithmetic: 60.7 us -> none  [the longest x2 21.3 us: causal_conv(): total = total + kernel[offset] * padded[:, offset:offset + length, :]]
    reshape x14 -> x3, local copies, waits for them, and re-layouts: 54.4 us -> 1.43 us  [the longest x1 0.72 us: local(): value_conv.reshape(-1)]
    psum x3 -> x0, blocking collectives: 51.1 us -> none  [the longest x1 41.2 us: local(): lax.psum((small[0], small[1], small[2], small[3], small[4], small[5], sma...]
  transfers between devices with their start and end apart: 15 -> 5, of which waited for: 9 -> 5; matrix products, arithmetic and copies ran while one was open for 26% -> 7% of each run, Pallas kernels for 0% -> 5%
where the time goes in v1:
time: 640 us; the launch traced here: 639 us
  waiting for transfers between devices  437 us (68%)
  Pallas kernels  125 us (20%)
  local copies, waits for them, and re-layouts  30.8 us (5%)
  other arithmetic  17.2 us (3%)
  between operations  13.9 us (2%)
  matrix products  9.1 us (1%)
    reduce_scatter x1, waiting for transfers between devices, local(): lax.psum_scatter(early.reshape(HALVES * width, -1), both, scatter_dimensi...  137 us
    reduce_scatter x1, waiting for transfers between devices, local(): lax.psum_scatter(late.reshape(HALVES * width, -1), both, scatter_dimensio...  118 us
    psum x1, waiting for transfers between devices, local(): lax.psum((taps_partial, head_partial, gain_partial, state_taps, prenorm_p...  100 us
    all_gather x2, waiting for transfers between devices, local(): lax.all_gather(pack, both, axis=0, tiled=True)  81.9 us
    pallas_call x1, Pallas kernels, local(): call(backward_kernel, (HALVES, blocks), [back((1, BLOCK, w)), back((1, BL...  49.1 us
    pallas_call x1, Pallas kernels, local(): call(gated_kernel, (blocks,), [tokens, tokens, row_block((BLOCK, width)),...  25.3 us
    pallas_call x1, Pallas kernels, local(): call(forward_kernel, (HALVES, blocks), [pl.BlockSpec((BLOCK, width), lamb...  24.7 us
  transfers between devices with their start and end apart: 5, of which 5 were waited for; matrix products, arithmetic and copies ran while one was open for 7% of the time, Pallas kernels for 5%

profile of v1, /device:TPU:0, one launch (start us, length us, event | category | flops | bytes accessed | tf_op | source)
XLA Modules:
  0.0 638.5 jit_solution(14637797943051883729)
XLA Ops:
  7.2 0.8 copy.54
  8.0 1.6 fusion.7
  9.6 0.0 all-gather.7.cloned.1.call-start
  9.6 1.6 pad_maximum_fusion.2
  11.3 0.7 reshape.74
  12.0 0.7 broadcast_in_dim.25
  12.8 0.1 reshape.75
  12.8 0.7 constant_dynamic-update-slice_fusion.4
  13.5 0.7 constant_dynamic-update-slice_fusion.2
  14.2 0.7 constant_dynamic-update-slice_fusion.1
  14.9 0.7 negate_bitcast_fusion
  15.6 5.4 all-gather.1
  21.0 1.3 broadcast_in_dim.23.gain_ref
  22.3 0.6 fusion.8
  22.9 0.6 copy.56
  23.5 0.6 copy.55
  24.1 0.6 reshape.78
  24.7 0.6 fusion.9
  25.3 48.9 %all-gather.5.cloned.1.call-done = bf16[1536,1152]{1,0:T(8,128)(2,1)} async-done(((bf16[48,1152]{1,0:T(8,128)(2,1)}), bf16[1536,1152]{1,0:T(8,128)(2,1)}) %all-gather.5.cloned.1.call-update) | async-done | bytes 3538960 | tf_op jit(solution)/shard_map/all_gather | solution.py:452
  74.2 8.2 %shard_map.279 = (bf16[1024,768]{1,0:T(8,128)(2,1)}, f32[1024,256]{1,0:T(8,128)}, f32[1024,256]{1,0:T(8,128)}, bf16[1024,256]{1,0:T(8,128)(2,1)}, bf16[256,1024]...) custom-call(bf16[1,1024,768]{2,1,0:T(8,128)(2,1)} %x_ref.5, ...), custom_call_target="tpu_custom_call" | custom-call | flops 805306368 | bytes 10000000 | tf_op jit(solution)/shard_map/pallas_call | solution.py:476
  82.4 24.7 %shard_map.280 = (bf16[2,1024,768]{2,1,0:T(8,128)(2,1)}, f32[2,1024,768]{2,1,0:T(8,128)}, f32[2,1024,768]{2,1,0:T(8,128)}, f32[2,4,128,768]{3,2,1,0:T(8,128)}) custom-call(bf16[1024,768]{1,0:T(8,128)(2,1)} %get-tuple-element.44.normed_ref, bf16[2,768,1152]{2,1,0:T(8,128)(2,1)} %bitcast.59, f32[4,1536]{1,0:T(4,128)} %bitcast.73, f32[1,1536]{1,0:T(1,128)} %bitcast.77, ...), custom_call_target="tpu_custom_call" | custom-call | flops 20000000000 | bytes 10000000 | tf_op jit(solution)/shard_map/pallas_call | solution.py:497
  107.1 33.0 %all-gather.7.cloned.1.call-done = bf16[1536,1536]{1,0:T(8,128)(2,1)} async-done(((bf16[48,1536]{1,0:T(8,128)(2,1)}), bf16[1536,1536]{1,0:T(8,128)(2,1)}) %all-gather.7.cloned.1.call-update) | async-done | bytes 4718608 | tf_op jit(solution)/shard_map/all_gather | solution.py:454
  140.1 25.3 %shard_map.281 = (bf16[1,1024,768]{2,1,0:T(8,128)(2,1)}, bf16[2,1024,768]{2,1,0:T(8,128)(2,1)}, bf16[2,1024,768]{2,1,0:T(8,128)(2,1)}, f32[2,768,768]{2,1,0:T(8,...) custom-call(bf16[1,1024,768]{2,1,0:T(8,128)(2,1)} %x_ref.5, bf16[1,1024,768]{2,1,0:T(8,128)(2,1)} %cot_ref.3, ...), custom_call_target="tpu_custom_call" | custom-call | flops 20000000000 | bytes 10000000 | tf_op jit(solution)/shard_map/pallas_call | solution.py:513
  165.4 49.1 %shard_map.282 = (bf16[2,1024,768]{2,1,0:T(8,128)(2,1)}, f32[2,1024,256]{2,1,0:T(8,128)}, bf16[2,1024,128]{2,1,0:T(8,128)(2,1)}, f32[2,8,768]{2,1,0:T(8,128)}, f32[2,8,128]{2,1,0:T(8,128)}) custom-call(f32[2,1024,768]{2,1,0:T(8,128)} %get-tuple-element.53.c_ref, bf16[2,1024,768]{2,1,0:T(8,128)(2,1)} %get-tuple-element.54.vin_ref, ...), custom_call_target="tpu_custom_call" | custom-call | flops 40000000000 | bytes 10000000 | tf_op jit(solution)/shard_map/pallas_call | solution.py:526
  214.5 6.8 %convolution_bitcast_fusion = f32[2,768,768]{1,2,0:T(8,128)} fusion(bf16[2,1024,768]{2,1,0:T(8,128)(2,1)} %get-tuple-element.58.dvin_ref, bf16[1024,768]{1,0:T(8,128)(2,1)S(1)} %copy-done), kind=kOutput, calls=%fused_computation.2 | convolution fusion | flops 2415919104 | bytes 9437184 | tf_op jit(solution)/shard_map/tk,htf->hkf/dot_general | solution.py:566
  221.3 5.4 shard_map.283
  226.7 1.7 fusion.10
  228.4 0.6 fusion.3
  229.0 12.2 %shard_map.284 = (f32[1,1024,768]{2,1,0:T(8,128)}, f32[8,768]{1,0:T(8,128)}) custom-call(bf16[1,1024,768]{2,1,0:T(8,128)(2,1)} %x_ref.5, bf16[1,1024,768]{2,1,0:T(8,128)(2,1)} %cot_ref.3, f32[1,768]{1,0:T(1,128)} %broadcast_in_dim.23.gain_ref, bf16[2,1024,768]{2,1,0:T(8,128)(2,1)} %get-tuple-element.52.dgate_ref, ...), custom_call_target="tpu_custom_call" | custom-call | flops 6000000000 | bytes 10000000 | tf_op jit(solution)/shard_map/pallas_call | solution.py:556
  241.3 0.1 broadcast_in_dim.28
  241.4 4.8 pad_maximum_fusion.1
  246.2 8.1 %copy.48 = f32[2,768,1152]{2,1,0:T(8,128)} copy(f32[2,768,1152]{1,2,0:T(8,128)} %pad_maximum_fusion.1) | data formatting | bytes 14155776 | tf_op jit(solution)/shard_map/concatenate | solution.py:569
  254.4 8.6 %pad_maximum_fusion = f32[2,768,1536]{2,1,0:T(8,128)} fusion(f32[2,768,768]{2,1,0:T(8,128)} %get-tuple-element.67, f32[2,768,768]{2,1,0:T(8,128)} %get-tuple-element.66), kind=kLoop, calls=%fused_computation | loop fusion | flops 2359296 | bytes 18874368 | tf_op jit(solution)/shard_map/concatenate | solution.py:572
  263.0 100.1 %all-reduce.6.cloned.1.call-done = (f32[8,768]{1,0:T(8,128)}, f32[2,8,768]{2,1,0:T(8,128)}, f32[8,256]{1,0:T(8,128)}, f32[2,8,128]{2,1,0:T(8,128)}, f32[2,768]{1,0:T(2,128)}) async-done(((f32[8,768]{1,0:T(8,128)}, f32[2,8,768]{2,1,0:T(8,128)}, f32[8,256]{1,0:T(8,128)}, f32[2,8,128]{2,1,0:T(8,128)}, f32[2,768]{1,0:T(2,128)}), (f32[8,768]{1,0:T(8,128)}, f32[2,8,768]{2,1,0:T(8,128)}, f32[8,256]{1,0:T(8,128)}, ...) | async-done | bytes 96272 | tf_op jit(solution)/shard_map/psum | solution.py:575
  363.1 1.3 slice.92
  364.4 1.3 slice.93
  365.6 1.3 dynamic-slice_reduce_fusion
  367.0 0.7 dynamic-slice_bitcast_fusion.1
  367.7 1.3 dynamic-slice_bitcast_fusion
  369.0 1.4 slice_reduce_fusion
  370.4 0.5 slice_bitcast_fusion.3
  370.9 117.9 %reduce-scatter.5.cloned.1.call-done = f32[48,1152]{1,0:T(8,128)} async-done(((f32[1536,1152]{1,0:T(8,128)}), f32[48,1152]{1,0:T(8,128)}) %reduce-scatter.5.cloned.1.call-update) | async-done | bytes 221200 | tf_op jit(solution)/shard_map/reduce_scatter | solution.py:573
  488.8 0.7 slice.91
  489.5 0.7 copy.49
  490.2 1.6 slice.89
  491.8 1.4 slice.90
  493.2 137.1 %reduce-scatter.3.cloned.1.call-done = f32[48,1536]{1,0:T(8,128)} async-done(((f32[1536,1536]{1,0:T(8,128)}), f32[48,1536]{1,0:T(8,128)}) %reduce-scatter.3.cloned.1.call-update) | async-done | bytes 294928 | tf_op jit(solution)/shard_map/reduce_scatter | solution.py:574
  630.3 1.7 slice_bitcast_fusion
  (19 shorter events, 0.3 us)
Async XLA Ops:
  7.2 67.0 %all-gather.5.cloned.1.call-start = ((), (), s32[]{:S(2)}) async-start(), calls=%async_computation.2 | async-start | bytes 3649536 | tf_op jit(solution)/shard_map/all_gather | solution.py:452
  9.6 130.5 %all-gather.7.cloned.1.call-start = ((), (), s32[]{:S(2)}) async-start(), calls=%async_computation.3 | async-start | bytes 4866048 | tf_op jit(solution)/shard_map/all_gather | solution.py:454
  11.3 351.8 %all-reduce.6.cloned.1.call-start = ((), (), s32[]{:S(2)}) async-start(), calls=%async_computation.6 | async-start | bytes 192512 | tf_op jit(solution)/shard_map/psum | solution.py:575
  165.4 49.2 %copy-start = (bf16[1024,768]{1,0:T(8,128)(2,1)S(1)}, bf16[1024,768]{1,0:T(8,128)(2,1)}, u32[]{:S(2)}) copy-start(bf16[1024,768]{1,0:T(8,128)(2,1)} %get-tuple-element.44.normed_ref) | copy-start | bytes 4718596
  226.7 1.7 copy-start.1
  241.3 247.5 %reduce-scatter.5.cloned.1.call-start = ((), (), s32[]{:S(2)}) async-start(), calls=%async_computation.5 | async-start | bytes 7299072 | tf_op jit(solution)/shard_map/reduce_scatter | solution.py:573
  254.3 376.0 %reduce-scatter.3.cloned.1.call-start = ((), (), s32[]{:S(2)}) async-start(), calls=%async_computation.4 | async-start | bytes 9732096 | tf_op jit(solution)/shard_map/reduce_scatter | solution.py:574
Sparse Core Ops, SparseCore 0:
  11.5 62.7 all-gather.4
  77.7 62.3 all-gather.6
  241.4 121.6 all-reduce.5
  368.6 120.1 reduce-scatter.4
  495.5 134.7 reduce-scatter.2
